TPU v7x, 32 devices: a whole 2x2x4 slice. The times are simulated.
32 devices in a mesh: tm: 8 (over z, y), chan: 4 (over x, core).
Axes of the slice: x: 2, y: 2, z: 4, core: 2. Of those that a mesh axis runs over, the one named last changes fastest.
Arguments:
- raw_strain: bfloat16 [512, 40960], P('chan', 'tm'), may hold values from -48 to 48
- fir_taps: float32 [128], replicated, may hold values from -0.5 to 0.5
- source_channels: int32 [32], replicated, may hold values from 0 to 511, as said below
- live_counts: int32 [32], P(('chan', 'tm')), may hold values from 8 to 16, as said below
Outputs:
- correlations: float32 [32, 512, 384], P(None, ('chan', 'tm'))
Inputs may be any that keep to these rules, and one draw needn't show every extreme that they name: `source_channels`: the virtual sources are distinct live channels; at most 2 of them lie in one aligned block of 16 channels, and some block holds exactly 2. `live_counts`: some block has all 16 channels live and some has exactly half of them.
All inputs are finite; a program needn't handle non-finite values.
Results may differ from a plain program's by a relative error of at most 0.015.
Values may be sent and summed in bfloat16 or wider, within the bound.
No kernel may reach another device: no remote copies, remote signals or barrier semaphores. Data moves between devices by JAX's collectives and lax.ppermute only.
A program may use at most 128 MiB of HBM per device.

v0:
```python
import functools
import math

import jax
import jax.numpy as jnp
import ml_dtypes
import numpy as np
from jax import lax
from jax.experimental import pallas as pl
from jax.experimental.pallas import tpu as pltpu
from jax.sharding import PartitionSpec as P

DECIM = 10
SEG = 1024
BAND = 64
LAGH = 192
SRC_DEV = 1
LANES = 128
HALF = SEG // 2
CHUNKS = HALF // LANES
EDGE = 14
PER_TILE = LANES // (3 * EDGE)
ROWS = 16
CORES = 2
MIB = 1024 * 1024

whiten_eps = 1e-06

NT = (((1,), (1,)), ((), ()))


def split_table(table):
    hi = table.astype(ml_dtypes.bfloat16)
    lo = (table - hi.astype(np.float64)).astype(ml_dtypes.bfloat16)
    return hi, lo


def dft_table(rows):
    phase = (np.arange(rows)[:, None] * np.arange(HALF)[None, :] % SEG) * (2.0 * np.pi / SEG)
    parts = []
    for j in range(CHUNKS):
        cut = slice(j * LANES, (j + 1) * LANES)
        hi, lo = split_table(np.concatenate([np.cos(phase[:, cut]), -np.sin(phase[:, cut])], 1))
        parts += [hi, lo]
    return np.concatenate(parts, axis=1)


def lag_table(seg_count):
    freq = np.arange(HALF)[:, None]
    phase = (freq * np.arange(-LAGH, LAGH)[None, :] % SEG) * (2.0 * np.pi / SEG)
    weight = np.where(freq == 0, 1.0, 2.0) * (math.sqrt(SEG / seg_count) / SEG)
    re = (weight * np.cos(phase)).reshape(CHUNKS, LANES, 2 * LAGH)
    im = (-weight * np.sin(phase)).reshape(CHUNKS, LANES, 2 * LAGH)
    return np.concatenate([re, im], axis=1).reshape(SEG, 2 * LAGH).astype(ml_dtypes.bfloat16)


def iota(shape, dim):
    return lax.broadcasted_iota(jnp.int32, shape, dim)


def one_hot(mask):
    return jnp.where(mask, 1.0, 0.0).astype(jnp.bfloat16)


def column(row):
    n = row.shape[1]
    return jnp.sum(jnp.where(iota((n, n), 0) == iota((n, n), 1), row, 0), axis=1, keepdims=True)


def tap_rows(taps):
    tap_count = taps.shape[1]
    width = 3 * LANES
    flip = one_hot(iota((tap_count, width), 0) + iota((tap_count, width), 1) == tap_count)
    hi = taps.astype(jnp.bfloat16)
    lo = (taps - hi.astype(jnp.float32)).astype(jnp.bfloat16)
    out = []
    for part in (hi, lo):
        base = jnp.dot(
            jnp.broadcast_to(part.astype(jnp.float32), (8, tap_count)).astype(jnp.bfloat16),
            flip,
            preferred_element_type=jnp.float32,
        )
        upper = pltpu.roll(base, 0, 1, stride=DECIM, stride_axis=0)
        out.append(jnp.concatenate([upper, pltpu.roll(upper, 8 * DECIM, 1)], axis=0))
    return out


def edge_tiles(count):
    return -(-count // (PER_TILE * ROWS))


def filter_kernel(
    blocks,
    src_hbm, taps_hbm, raw_ref, tab_hbm,
    out_ref, slot_ref, tab_ref,
    ext, weight, src_ref, taps_ref, sems,
):
    rows, raw_len = raw_ref.shape
    steps = out_ref.shape[0]
    ch = rows // steps
    span = raw_len // blocks
    wide = span + LANES
    copies = []
    for b in range(blocks):
        if b == 0:
            copy = pltpu.make_async_copy(
                raw_ref.at[:, pl.ds(0, span)],
                ext.at[pl.ds(0, rows), pl.ds(LANES, span)],
                sems.at[b],
            )
        else:
            copy = pltpu.make_async_copy(
                raw_ref.at[:, pl.ds(b * span - LANES, wide)],
                ext.at[pl.ds(b * rows, rows), :],
                sems.at[b],
            )
        copy.start()
        copies.append(copy)
    small = [
        pltpu.make_async_copy(taps_hbm, taps_ref, sems.at[blocks]),
        pltpu.make_async_copy(src_hbm, src_ref, sems.at[blocks + 1]),
    ]
    tables = pltpu.make_async_copy(tab_hbm, tab_ref, sems.at[blocks + 2])
    for copy in [*small, tables]:
        copy.start()
    ext[:rows, :LANES] = jnp.zeros((rows, LANES), ext.dtype)
    weight[...] = jnp.zeros_like(weight)
    for copy in small:
        copy.wait()
    for p, base in enumerate(tap_rows(taps_ref[...])):
        for i in range(LANES // 16):
            tile, lane = divmod(16 * DECIM * i, LANES)
            piece = pltpu.roll(base, lane, 1) if lane else base
            weight[p * LANES + 16 * i : p * LANES + 16 * (i + 1), tile * LANES : (tile + 3) * LANES] = (
                piece.astype(jnp.bfloat16)
            )
    src = src_ref[...]
    src_count = src.shape[1]
    slots = slot_ref.shape[0]
    group = src // rows
    group_col = column(group)
    src_col = column(src)
    rank = jnp.sum(
        jnp.where(
            (group_col == group)
            & (iota((src_count, src_count), 0) < iota((src_count, src_count), 1)),
            1,
            0,
        ),
        axis=0,
        keepdims=True,
    )
    mine = lax.axis_index("chan")
    to_slot = one_hot((iota((slots, src_count), 0) == rank) & (group == mine))
    to_row = one_hot(src_col - mine * rows == iota((src_count, rows), 1))
    pick = jnp.dot(to_slot, to_row, preferred_element_type=jnp.float32).astype(jnp.bfloat16)
    number = jnp.where(
        iota((src_count, LANES), 1) == LANES - 1, iota((src_count, LANES), 0) + 1, 0
    ).astype(jnp.float32).astype(jnp.bfloat16)
    number = jnp.dot(to_slot, number, preferred_element_type=jnp.float32)
    for copy in copies:
        copy.wait()
    acc = lax.dot_general(ext[...], weight[...], NT, preferred_element_type=jnp.float32)
    acc = acc[:, :LANES] + acc[:, LANES:]
    y = acc.astype(jnp.bfloat16)
    head = acc[:rows]
    head_lo = head - head.astype(jnp.bfloat16).astype(jnp.float32)
    tail = lax.dot_general(
        ext[(blocks - 1) * rows :, wide - LANES :], weight[:, :LANES], NT,
        preferred_element_type=jnp.float32,
    )
    tail = tail[:, :LANES] + tail[:, LANES:]
    tail_hi = tail.astype(jnp.bfloat16).astype(jnp.float32)
    lane = iota((rows, LANES), 1)
    edge = jnp.where(
        lane < EDGE,
        head_lo,
        jnp.where(
            lane < 2 * EDGE,
            pltpu.roll(tail_hi, EDGE, 1),
            jnp.where(lane < 3 * EDGE, pltpu.roll(tail - tail_hi, 2 * EDGE, 1), 0.0),
        ),
    ).astype(jnp.bfloat16)
    parts = [y[b * rows : (b + 1) * rows] for b in range(blocks)] + [edge]
    last = blocks * ch
    for t in range(steps):
        for b in range(blocks):
            out_ref[t, b * ch : (b + 1) * ch] = parts[b][t * ch : (t + 1) * ch]
        out_ref[t, last : last + ch] = edge[t * ch : (t + 1) * ch]
    for b, part in enumerate(parts):
        found = jnp.dot(pick, part, preferred_element_type=jnp.float32)
        if b == blocks:
            found += number
        slot_ref[:, b * LANES : (b + 1) * LANES] = found.astype(jnp.bfloat16)
    tables.wait()


def arrange_kernel(half, blocks, pieces, *refs):
    slots = jnp.concatenate([ref[...] for ref in refs[:pieces]], axis=0)
    part_ref, *out_refs = refs[pieces:]
    height = out_refs[0].shape[0]
    own_rows = part_ref.shape[1] - ROWS
    tile_rows = height - 2 * own_rows - blocks * half
    numbers = slots[:, blocks * LANES :].astype(jnp.float32)
    total = numbers.shape[0]
    numbers = jnp.sum(
        jnp.where(iota((total, LANES), 1) == LANES - 1, numbers, 0.0), axis=1, keepdims=True
    ).astype(jnp.int32)
    first = lax.axis_index("chan") % CORES * half
    pick = one_hot(numbers == iota((total, half), 1) + 1 + first)
    found = lax.dot_general(
        pick, slots, (((0,), (0,)), ((), ())), preferred_element_type=jnp.float32
    )
    fill = [found[:, b * LANES : (b + 1) * LANES].astype(jnp.bfloat16) for b in range(blocks)]
    edges = jnp.where(iota((half, LANES), 1) < 3 * EDGE, found[:, blocks * LANES :], 0.0)
    added = [jnp.zeros((ROWS, LANES), jnp.float32) for _ in range(tile_rows // ROWS)]
    for i in range(half // ROWS):
        tile, place = divmod(i + 2, PER_TILE)
        piece = edges[i * ROWS : (i + 1) * ROWS]
        added[tile] += pltpu.roll(piece, 3 * EDGE * place, 1) if place else piece
    me = lax.axis_index("tm")
    *out_refs, direct_ref = out_refs
    for k, out_ref in enumerate(out_refs):
        same = part_ref[me ^ (2 * k)]
        other = part_ref[me ^ (2 * k) ^ 1]
        mixed = same[own_rows:].astype(jnp.float32) + pltpu.roll(
            other[own_rows:].astype(jnp.float32), 3 * EDGE, 1
        )
        if k == 1:
            writes = [(out_ref, [same]), (direct_ref, [other])]
        else:
            writes = [(out_ref, [same, other])]
        for ref, owners in writes:
            at = 0
            for owner in owners:
                ref[at : at + own_rows] = owner[:own_rows]
                at += own_rows
            for piece in fill:
                ref[at : at + half] = piece
                at += half
            for tile, extra in enumerate(added):
                ref[at : at + ROWS] = (extra + mixed if tile == 0 else extra).astype(jnp.bfloat16)
                at += ROWS


def forward_kernel(own_rows, block_ref, out_ref):
    out_ref[...] = block_ref[own_rows:]


def direct_first(refs):
    return [refs[1], refs[0], *refs[2:]]


def collect_kernel(own_rows, *refs):
    *block_refs, out_ref = refs
    highs = len(block_refs) // 2
    passed_refs = direct_first(block_refs[highs:])
    me = lax.axis_index("tm")
    for k in range(highs):
        out_ref[me ^ (2 * k)] = block_refs[k][block_refs[k].shape[0] - out_ref.shape[1] :]
        out_ref[me ^ (2 * k) ^ 1] = passed_refs[k][own_rows:]


def correlate_kernel(
    seg_count, src_count, dec, head_len, part_rows, count, steps, live_ref, tab_ref, *refs
):
    count_high = steps // 2
    block_refs, passed_refs = refs[:count_high], direct_first(refs[count_high:steps])
    given_ref, far_ref, out_ref = refs[steps : steps + 3]
    mine_ref, mine_edge, trace, own, other, cross, result, sems = refs[steps + 3 :]
    ch = out_ref.shape[1]
    own_rows = mine_ref.shape[1]
    half = src_count // CORES
    rows = ch + src_count
    per_seg = SEG // dec
    blocks = dec // LANES
    d_cols = 4 * HALF

    @pl.when(pl.program_id(0) == 0)
    def _():
        me = lax.axis_index("tm")
        last = block_refs[0].shape[0] - edge_tiles(2 * ch + half) * ROWS
        for k, ref in enumerate(block_refs):
            mine_ref[me ^ (2 * k)] = ref[:own_rows]
            at = ref.shape[0] - (block_refs[0].shape[0] - last)
            mine_edge[me ^ (2 * k)] = ref[at : at + ROWS].astype(jnp.float32)
        for k, ref in enumerate(passed_refs):
            mine_ref[me ^ (2 * k) ^ 1] = ref[:own_rows]
            pack = ref[last - own_rows : last - own_rows + ROWS].astype(jnp.float32)
            mine_edge[me ^ (2 * k) ^ 1] = pltpu.roll(pack, LANES - 3 * EDGE, 1)
        live = iota((ch, LANES), 0) < live_ref[0]
        before = jnp.zeros((rows, LANES), jnp.float32)
        is_head = iota((rows, LANES), 1) < head_len
        tile_rows = edge_tiles(2 * ch + half) * ROWS
        low_core = lax.axis_index("chan") % CORES == 0

        def edge_groups(ref, t):
            out = []
            last = ref.shape[1] - tile_rows
            for i in range(2, 2 + half // ROWS):
                tile, place = divmod(i, PER_TILE)
                pack = ref[t, last + tile * ROWS : last + (tile + 1) * ROWS].astype(jnp.float32)
                out.append(pltpu.roll(pack, LANES - 3 * EDGE * place, 1) if place else pack)
            return jnp.concatenate(out, axis=0)

        def in_order(near, far):
            return [jnp.where(low_core, near, far), jnp.where(low_core, far, near)]

        for t in range(steps):
            edge = jnp.where(live, mine_edge[t], 0.0)
            theirs = edge_groups(given_ref, t), edge_groups(far_ref, t)
            edge = jnp.concatenate([edge, *in_order(*theirs)], axis=0)
            for b in range(blocks):
                mine = mine_ref[t, b * ch : (b + 1) * ch]
                mine = jnp.where(live, mine, jnp.zeros_like(mine))
                rows_b = slice(b * half, (b + 1) * half)
                theirs = given_ref[t, rows_b], far_ref[t, rows_b]
                both = jnp.concatenate([mine, *in_order(*theirs)], axis=0)
                if b == 0:
                    tail = pltpu.roll(before, LANES - EDGE, 1) + pltpu.roll(before, LANES - 2 * EDGE, 1)
                    both = both.astype(jnp.float32)
                    both = jnp.where(is_head, both + edge + tail, both).astype(jnp.bfloat16)
                trace[t * rows : (t + 1) * rows, b * LANES : (b + 1) * LANES] = both
            before = edge
        odd = (iota((rows, 2 * LANES), 1) & 1) == 1
        sign = jnp.where(odd, -1.0, 1.0)
        same = one_hot(
            iota((2 * LANES, LANES), 0) % LANES // BAND == iota((2 * LANES, LANES), 1) // BAND
        )
        group_segs = max(1, min(seg_count, part_rows // (per_seg * rows)))
        for first in range(0, seg_count, group_segs):
            segs = min(group_segs, seg_count - first)
            lhs = trace[first * per_seg * rows : (first + segs) * per_seg * rows, :]
            for j in range(CHUNKS):
                acc = jnp.dot(
                    lhs, tab_ref[:, 4 * j * LANES : 4 * (j + 1) * LANES],
                    preferred_element_type=jnp.float32,
                )
                folded = acc[:, : 2 * LANES] + acc[:, 2 * LANES :]
                spec = []
                for g in range(segs):
                    a = folded[g * per_seg * rows : (g * per_seg + 1) * rows]
                    b = folded[(g * per_seg + 1) * rows : (g * per_seg + 2) * rows]
                    spec.append(a + sign * b)
                spec = jnp.concatenate(spec, axis=0)
                re, im = spec[:, :LANES], spec[:, LANES:]
                power = re * re + im * im
                hi = power.astype(jnp.bfloat16)
                lo = (power - hi.astype(jnp.float32)).astype(jnp.bfloat16)
                total = jnp.dot(
                    jnp.concatenate([hi, lo], axis=1), same, preferred_element_type=jnp.float32
                )
                scale = lax.rsqrt(total * (1.0 / BAND) + whiten_eps)
                w_re = (re * scale).astype(jnp.bfloat16).astype(jnp.float32)
                w_im = (im * scale).astype(jnp.bfloat16).astype(jnp.float32)
                at = 2 * j * LANES
                for g in range(segs):
                    r, o = g * rows, (first + g) * ch
                    own[o : o + ch, at : at + LANES] = w_re[r : r + ch]
                    own[o : o + ch, at + LANES : at + 2 * LANES] = w_im[r : r + ch]
                    o = (first + g) * src_count
                    other[o : o + src_count, at : at + LANES] = w_re[r + ch : r + rows]
                    other[o : o + src_count, at + LANES : at + 2 * LANES] = w_im[r + ch : r + rows]

    block = cross.shape[1] // ch
    copies = []
    for i in range(count):
        start = pl.multiple_of((pl.program_id(0) * count + i) * block, 8)
        for j in range(CHUNKS):
            at = 2 * j * LANES
            a_re = [own[g * ch : (g + 1) * ch, at : at + LANES] for g in range(seg_count)]
            a_im = [own[g * ch : (g + 1) * ch, at + LANES : at + 2 * LANES] for g in range(seg_count)]
            for s in range(block):
                if s % 8 == 0:
                    tiles = [
                        other[
                            pl.ds(pl.multiple_of(g * src_count + start + s, 8), 8),
                            at : at + 2 * LANES,
                        ]
                        for g in range(seg_count)
                    ]
                re = im = None
                for g in range(seg_count):
                    b_re = tiles[g][s % 8 : s % 8 + 1, :LANES]
                    b_im = tiles[g][s % 8 : s % 8 + 1, LANES:]
                    p = a_re[g] * b_re + a_im[g] * b_im
                    q = a_im[g] * b_re - a_re[g] * b_im
                    re, im = (p, q) if re is None else (re + p, im + q)
                row = slice(s * ch, (s + 1) * ch)
                cross[i, row, at : at + LANES] = re.astype(jnp.bfloat16)
                cross[i, row, at + LANES : at + 2 * LANES] = im.astype(jnp.bfloat16)
        lags = sum(
            jnp.dot(
                cross[i, :, h * dec : (h + 1) * dec],
                tab_ref[:, d_cols + 2 * LAGH * h : d_cols + 2 * LAGH * (h + 1)],
                preferred_element_type=jnp.float32,
            )
            for h in range(per_seg)
        )
        result[i] = lags.reshape(result.shape[1:])
        copy = pltpu.make_async_copy(result.at[i], out_ref.at[pl.ds(start, block)], sems.at[i])
        copy.start()
        copies.append(copy)
    for copy in copies:
        copy.wait()


def whole(space=pltpu.VMEM):
    return pl.BlockSpec(memory_space=space)


def local(raw_strain, fir_taps, source_channels, live_counts):
    rows, raw_len = raw_strain.shape
    steps = lax.axis_size("tm")
    chan_count = lax.axis_size("chan")
    dec = raw_len // DECIM
    blocks = dec // LANES
    ch = rows // steps
    seg_count = steps * dec // SEG
    src_count = source_channels.shape[0]
    slots = 2 * SRC_DEV * steps
    span = raw_len // blocks
    total_rows = ch + src_count
    half = src_count // CORES
    highs = steps // 2
    own_rows = blocks * ch
    given_rows = blocks * half + edge_tiles(2 * ch + half) * ROWS
    height = 2 * own_rows + given_rows
    head_len = -(-(fir_taps.shape[0] - 1) // DECIM)
    assert head_len < EDGE and ch == ROWS and src_count <= 256
    assert steps >= 8 and steps & (steps - 1) == 0 and chan_count & (chan_count - 1) == 0 and half % ROWS == 0
    src = source_channels.reshape(1, src_count)
    taps = fir_taps.reshape(1, fir_taps.shape[0])
    table = np.concatenate([dft_table(dec), *lag_table(seg_count).reshape(SEG // dec, dec, -1)], axis=1)
    inputs = (src, taps, raw_strain, jnp.asarray(table))
    part, picked, table = pl.pallas_call(
        functools.partial(filter_kernel, blocks),
        out_shape=[
            pltpu.VMEM((steps, (blocks + 1) * ch, LANES), jnp.bfloat16),
            pltpu.VMEM((slots, dec + LANES), jnp.bfloat16),
            pltpu.VMEM(table.shape, jnp.bfloat16),
        ],
        in_specs=[whole(pl.ANY)] * 4,
        out_specs=[whole(), whole(), whole(pl.ANY)],
        scratch_shapes=[
            pltpu.VMEM((blocks * rows, span + LANES), jnp.bfloat16),
            pltpu.VMEM((2 * LANES, span + LANES), jnp.bfloat16),
            pltpu.VMEM(src.shape, src.dtype),
            pltpu.VMEM(taps.shape, taps.dtype),
            pltpu.SemaphoreType.DMA((blocks + 3,)),
        ],
        compiler_params=pltpu.CompilerParams(vmem_limit_bytes=16 * MIB),
        name="fir",
    )(*(pltpu.with_memory_space_constraint(a, pltpu.HBM) for a in inputs))
    pieces = [picked] + [
        lax.ppermute(picked, "chan", [(c, c ^ k) for c in range(chan_count)])
        for k in range(1, chan_count)
    ]
    to_vmem = functools.partial(pltpu.with_memory_space_constraint, memory_space=pltpu.VMEM)
    outgoing = pl.pallas_call(
        functools.partial(arrange_kernel, half, blocks, chan_count),
        out_shape=[
            pltpu.VMEM((rows_k, LANES), jnp.bfloat16)
            for rows_k in [height, height - own_rows, *[height] * (highs - 2), height - own_rows]
        ],
        in_specs=[whole()] * (chan_count + 1),
        out_specs=[whole()] * (highs + 1),
        compiler_params=pltpu.CompilerParams(vmem_limit_bytes=8 * MIB),
        name="arrange",
    )(*(to_vmem(a) for a in (*pieces, part)))
    arrived = [
        lax.ppermute(outgoing[k], "tm", [(t, t ^ (2 * k)) for t in range(steps)])
        for k in range(highs - 1, 0, -1)
    ]
    arrived = [to_vmem(a) for a in (outgoing[0], *arrived[::-1])]
    small = pltpu.CompilerParams(vmem_limit_bytes=8 * MIB)
    passed = [None] * highs
    for k in [1, 0, *range(highs - 1, 1, -1)]:
        if k == 1:
            forward, by = outgoing[highs], 3
        else:
            by = 1
            forward = pl.pallas_call(
                functools.partial(forward_kernel, own_rows),
                out_shape=pltpu.VMEM((own_rows + given_rows, LANES), jnp.bfloat16),
                in_specs=[whole()],
                out_specs=whole(),
                compiler_params=small,
                name="forward",
            )(arrived[k])
        passed[k] = to_vmem(lax.ppermute(forward, "tm", [(t, t ^ by) for t in range(steps)]))
    passed = direct_first(passed)
    given = pl.pallas_call(
        functools.partial(collect_kernel, own_rows),
        out_shape=pltpu.VMEM((steps, given_rows, LANES), jnp.bfloat16),
        in_specs=[whole()] * steps,
        out_specs=whole(),
        compiler_params=small,
        name="collect",
    )(*arrived, *passed)
    swapped = lax.ppermute(given, "chan", [(c, c ^ 1) for c in range(chan_count)])
    block = math.gcd(src_count, 16)
    count = math.gcd(src_count // block, 2)
    state = seg_count * total_rows * SEG * 4
    return pl.pallas_call(
        functools.partial(
            correlate_kernel, seg_count, src_count, dec, head_len, 1024, count, steps
        ),
        grid=(src_count // (block * count),),
        out_shape=jax.ShapeDtypeStruct((src_count, ch, 2 * LAGH), jnp.float32),
        in_specs=[whole(pltpu.SMEM)] + [whole()] * (steps + 3),
        out_specs=whole(pl.ANY),
        scratch_shapes=[
            pltpu.VMEM((steps, own_rows, LANES), jnp.bfloat16),
            pltpu.VMEM((steps, ROWS, LANES), jnp.float32),
            pltpu.VMEM((steps * total_rows, dec), jnp.bfloat16),
            pltpu.VMEM((seg_count * ch, SEG), jnp.float32),
            pltpu.VMEM((seg_count * src_count, SEG), jnp.float32),
            pltpu.VMEM((count, block * ch, SEG), jnp.bfloat16),
            pltpu.VMEM((count, block, ch, 2 * LAGH), jnp.float32),
            pltpu.SemaphoreType.DMA((count,)),
        ],
        compiler_params=pltpu.CompilerParams(vmem_limit_bytes=16 * MIB + 2 * state),
        name="correlate",
    )(live_counts, table, *arrived, *passed, to_vmem(given), to_vmem(swapped))


def solution(mesh):
    placed = (P("chan", "tm"), P(), P(), P(("chan", "tm")))
    return jax.shard_map(
        local, mesh=mesh, in_specs=placed, out_specs=P(None, ("chan", "tm"), None), check_vma=False
    )
```

profile of v0, /device:TPU:0, one launch (start us, length us, event | category | flops | bytes accessed | tf_op | source)
XLA Modules:
  0.0 27.2 jit_solution(3997326297309215239)
XLA Ops:
  0.0 2.4 %fir.1 = (bf16[8,80,128]{2,1,0:T(8,128)(2,1)S(1)}, bf16[16,640]{1,0:T(8,128)(2,1)S(1)}, bf16[512,2816]{1,0:T(8,128)(2,1)S(1)}) custom-call(s32[1,32]{1,0:T(1,128)} %bitcast.2, f32[1,128]{1,0:T(1,128)} %bitcast.3, bf16[128,5120]{1,0:T(8,128)(2,1)} %raw_ref.1, bf16[512,2816]{1,0:T(8,128)(2,1)} %constant.2.clone.tab_hbm), custom_call_target="tpu_custom_call" | custom-call | tf_op jit(solution)/shard_map/fir/pallas_call | solution.py:436
  2.4 2.4 %collective-permute-start.2 = (bf16[16,640]{1,0:T(8,128)(2,1)S(1)}, bf16[16,640]{1,0:T(8,128)(2,1)S(1)}, u32[]{:S(2)}, u32[]{:S(2)}) collective-permute-start(bf16[16,640]{1,0:T(8,128)(2,1)S(1)} %get-tuple-element.14.refs_0_), channel_id=1, source_target_pairs={{0,3},{1,2},{2,1},{3,0},{4,7},{5,6},{6,5},{7,4},{8,11},{9,10},{10,... | collective-permute-start | bytes 61448 | tf_op jit(solution)/shard_map/ppermute | solution.py:456
  4.8 0.6 %collective-permute-start.1 = (bf16[16,640]{1,0:T(8,128)(2,1)S(1)}, bf16[16,640]{1,0:T(8,128)(2,1)S(1)}, u32[]{:S(2)}, u32[]{:S(2)}) collective-permute-start(bf16[16,640]{1,0:T(8,128)(2,1)S(1)} %get-tuple-element.14.refs_0_), channel_id=1, source_target_pairs={{0,2},{1,3},{2,0},{3,1},{4,6},{5,7},{6,4},{7,5},{8,10},{9,11},{10,... | collective-permute-start | bytes 61448 | tf_op jit(solution)/shard_map/ppermute | solution.py:456
  5.4 0.0 collective-permute-start
  5.5 0.8 %collective-permute-done.2.refs_3_ = bf16[16,640]{1,0:T(8,128)(2,1)S(1)} collective-permute-done((bf16[16,640]{1,0:T(8,128)(2,1)S(1)}, bf16[16,640]{1,0:T(8,128)(2,1)S(1)}, u32[]{:S(2)}, u32[]{:S(2)}) %collective-permute-start.2) | collective-permute-done | bytes 20512 | tf_op jit(solution)/shard_map/ppermute | solution.py:456
  6.3 2.3 %collective-permute-done.1.refs_2_ = bf16[16,640]{1,0:T(8,128)(2,1)S(1)} collective-permute-done((bf16[16,640]{1,0:T(8,128)(2,1)S(1)}, bf16[16,640]{1,0:T(8,128)(2,1)S(1)}, u32[]{:S(2)}, u32[]{:S(2)}) %collective-permute-start.1) | collective-permute-done | bytes 20512 | tf_op jit(solution)/shard_map/ppermute | solution.py:456
  8.6 0.0 collective-permute-done.refs_1_
  8.6 0.3 %arrange.1 = (bf16[208,128]{1,0:T(8,128)(2,1)S(1)}, bf16[144,128]{1,0:T(8,128)(2,1)S(1)}, bf16[208,128]{1,0:T(8,128)(2,1)S(1)}, bf16[208,128]{1,0:T(8,128)(2,1)S(1)}, bf16[144,128]{1,0:T(8,128)(2,1)S(1)}) custom-call(bf16[16,640]{1,0:T(8,128)(2,1)S(1)} %get-tuple-element.14.refs_0_, bf16[16,640]{1,0:T(8,128)(2,1)S(1)} %collective-permute-done.refs_1_, ...), custom_call_target="tpu_custom_call" | custom-call | tf_op jit(solution)/shard_map/arrange/pallas_call | solution.py:460
  8.9 2.6 %collective-permute-start.4 = (bf16[208,128]{1,0:T(8,128)(2,1)S(1)}, bf16[208,128]{1,0:T(8,128)(2,1)S(1)}, u32[]{:S(2)}, u32[]{:S(2)}) collective-permute-start(bf16[208,128]{1,0:T(8,128)(2,1)S(1)} %get-tuple-element.18), channel_id=1, source_target_pairs={{0,16},{4,20},{8,24},{12,28},{16,0},{20,4},{24,8},{28,12},{1,17},{... | collective-permute-start | bytes 159752 | tf_op jit(solution)/shard_map/ppermute | solution.py:472
  11.5 1.3 %collective-permute-start.5 = (bf16[208,128]{1,0:T(8,128)(2,1)S(1)}, bf16[208,128]{1,0:T(8,128)(2,1)S(1)}, u32[]{:S(2)}, u32[]{:S(2)}) collective-permute-start(bf16[208,128]{1,0:T(8,128)(2,1)S(1)} %get-tuple-element.19), channel_id=1, source_target_pairs={{0,24},{4,28},{8,16},{12,20},{16,8},{20,12},{24,0},{28,4},{1,25},{... | collective-permute-start | bytes 159752 | tf_op jit(solution)/shard_map/ppermute | solution.py:472
  12.9 1.5 %collective-permute-start.7 = (bf16[144,128]{1,0:T(8,128)(2,1)S(1)}, bf16[144,128]{1,0:T(8,128)(2,1)S(1)}, u32[]{:S(2)}, u32[]{:S(2)}) collective-permute-start(bf16[144,128]{1,0:T(8,128)(2,1)S(1)} %forward.3), channel_id=1, source_target_pairs={{0,4},{4,0},{8,12},{12,8},{16,20},{20,16},{24,28},{28,24},{1,5},{5... | collective-permute-start | bytes 110600 | tf_op jit(solution)/shard_map/ppermute | solution.py:491
  14.4 0.2 collective-permute-start.3
  14.6 1.7 %collective-permute-start.6 = (bf16[144,128]{1,0:T(8,128)(2,1)S(1)}, bf16[144,128]{1,0:T(8,128)(2,1)S(1)}, u32[]{:S(2)}, u32[]{:S(2)}) collective-permute-start(bf16[144,128]{1,0:T(8,128)(2,1)S(1)} %get-tuple-element.20), channel_id=1, source_target_pairs={{0,12},{4,8},{8,4},{12,0},{16,28},{20,24},{24,20},{28,16},{1,13},{... | collective-permute-start | bytes 110600 | tf_op jit(solution)/shard_map/ppermute | solution.py:491
  16.4 0.0 collective-permute-done.4.block_ref.refs_2_
  16.4 1.5 %collective-permute-start.8 = (bf16[144,128]{1,0:T(8,128)(2,1)S(1)}, bf16[144,128]{1,0:T(8,128)(2,1)S(1)}, u32[]{:S(2)}, u32[]{:S(2)}) collective-permute-start(bf16[144,128]{1,0:T(8,128)(2,1)S(1)} %forward.4), channel_id=1, source_target_pairs={{0,4},{4,0},{8,12},{12,8},{16,20},{20,16},{24,28},{28,24},{1,5},{5... | collective-permute-start | bytes 110600 | tf_op jit(solution)/shard_map/ppermute | solution.py:491
  17.9 0.0 collective-permute-done.5.block_ref.refs_3_
  17.9 1.1 %collective-permute-start.9 = (bf16[144,128]{1,0:T(8,128)(2,1)S(1)}, bf16[144,128]{1,0:T(8,128)(2,1)S(1)}, u32[]{:S(2)}, u32[]{:S(2)}) collective-permute-start(bf16[144,128]{1,0:T(8,128)(2,1)S(1)} %forward.5), channel_id=1, source_target_pairs={{0,4},{4,0},{8,12},{12,8},{16,20},{20,16},{24,28},{28,24},{1,5},{5... | collective-permute-start | bytes 110600 | tf_op jit(solution)/shard_map/ppermute | solution.py:491
  19.0 0.0 collective-permute-done.7.refs_5_
  19.0 0.0 collective-permute-done.3.refs_1_
  19.0 0.4 %collective-permute-done.6.refs_4_ = bf16[144,128]{1,0:T(8,128)(2,1)S(1)} collective-permute-done((bf16[144,128]{1,0:T(8,128)(2,1)S(1)}, bf16[144,128]{1,0:T(8,128)(2,1)S(1)}, u32[]{:S(2)}, u32[]{:S(2)}) %collective-permute-start.6) | collective-permute-done | bytes 36896 | tf_op jit(solution)/shard_map/ppermute | solution.py:491
  19.5 0.8 %collective-permute-done.8.refs_6_ = bf16[144,128]{1,0:T(8,128)(2,1)S(1)} collective-permute-done((bf16[144,128]{1,0:T(8,128)(2,1)S(1)}, bf16[144,128]{1,0:T(8,128)(2,1)S(1)}, u32[]{:S(2)}, u32[]{:S(2)}) %collective-permute-start.8) | collective-permute-done | bytes 36896 | tf_op jit(solution)/shard_map/ppermute | solution.py:491
  20.3 1.5 %collective-permute-done.9.refs_7_ = bf16[144,128]{1,0:T(8,128)(2,1)S(1)} collective-permute-done((bf16[144,128]{1,0:T(8,128)(2,1)S(1)}, bf16[144,128]{1,0:T(8,128)(2,1)S(1)}, u32[]{:S(2)}, u32[]{:S(2)}) %collective-permute-start.9) | collective-permute-done | bytes 36896 | tf_op jit(solution)/shard_map/ppermute | solution.py:491
  21.9 0.1 collective-permute-start.10
  22.6 0.7 %collective-permute-done.10.refs_9_ = bf16[8,80,128]{2,1,0:T(8,128)(2,1)S(1)} collective-permute-done((bf16[8,80,128]{2,1,0:T(8,128)(2,1)S(1)}, bf16[8,80,128]{2,1,0:T(8,128)(2,1)S(1)}, u32[]{:S(2)}, u32[]{:S(2)}) %collective-permute-start.10) | collective-permute-done | bytes 163872 | tf_op jit(solution)/shard_map/ppermute | solution.py:501
  23.3 3.9 %correlate.1 = f32[32,16,384]{2,1,0:T(8,128)} custom-call(s32[1]{0:T(128)S(6)} %copy.6.live_ref, bf16[512,2816]{1,0:T(8,128)(2,1)S(1)} %get-tuple-element.13.tab_ref, bf16[208,128]{1,0:T(8,128)(2,1)S(1)} %get-tuple-element.16.block_ref.refs_0_, bf16[144,128]{1,0:T(8,128)(2,1)S(1)} %collective-permute-done.3.refs_1_, ...), custom_call_target="tpu_custom_call" | custom-call | tf_op jit(solution)/shard_map/correlate/pallas_call | solution.py:505
  (4 shorter events, 0.0 us)
Async XLA Ops:
  2.4 4.0 %collective-permute-start.2 = (bf16[16,640]{1,0:T(8,128)(2,1)S(1)}, bf16[16,640]{1,0:T(8,128)(2,1)S(1)}, u32[]{:S(2)}, u32[]{:S(2)}) collective-permute-start(bf16[16,640]{1,0:T(8,128)(2,1)S(1)} %get-tuple-element.14.refs_0_), channel_id=1, source_target_pairs={{0,3},{1,2},{2,1},{3,0},{4,7},{5,6},{6,5},{7,4},{8,11},{9,10},{10,... | collective-permute-start | bytes 61448 | tf_op jit(solution)/shard_map/ppermute | solution.py:456
  4.8 3.8 %collective-permute-start.1 = (bf16[16,640]{1,0:T(8,128)(2,1)S(1)}, bf16[16,640]{1,0:T(8,128)(2,1)S(1)}, u32[]{:S(2)}, u32[]{:S(2)}) collective-permute-start(bf16[16,640]{1,0:T(8,128)(2,1)S(1)} %get-tuple-element.14.refs_0_), channel_id=1, source_target_pairs={{0,2},{1,3},{2,0},{3,1},{4,6},{5,7},{6,4},{7,5},{8,10},{9,11},{10,... | collective-permute-start | bytes 61448 | tf_op jit(solution)/shard_map/ppermute | solution.py:456
  5.4 3.1 %collective-permute-start = (bf16[16,640]{1,0:T(8,128)(2,1)S(1)}, bf16[16,640]{1,0:T(8,128)(2,1)S(1)}, u32[]{:S(2)}, u32[]{:S(2)}) collective-permute-start(bf16[16,640]{1,0:T(8,128)(2,1)S(1)} %get-tuple-element.14.refs_0_), channel_id=1, source_target_pairs={{0,1},{1,0},{2,3},{3,2},{4,5},{5,4},{6,7},{7,6},{8,9},{9,8},{10,11... | collective-permute-start | bytes 61448 | tf_op jit(solution)/shard_map/ppermute | solution.py:456
  8.9 7.4 %collective-permute-start.4 = (bf16[208,128]{1,0:T(8,128)(2,1)S(1)}, bf16[208,128]{1,0:T(8,128)(2,1)S(1)}, u32[]{:S(2)}, u32[]{:S(2)}) collective-permute-start(bf16[208,128]{1,0:T(8,128)(2,1)S(1)} %get-tuple-element.18), channel_id=1, source_target_pairs={{0,16},{4,20},{8,24},{12,28},{16,0},{20,4},{24,8},{28,12},{1,17},{... | collective-permute-start | bytes 159752 | tf_op jit(solution)/shard_map/ppermute | solution.py:472
  11.5 6.4 %collective-permute-start.5 = (bf16[208,128]{1,0:T(8,128)(2,1)S(1)}, bf16[208,128]{1,0:T(8,128)(2,1)S(1)}, u32[]{:S(2)}, u32[]{:S(2)}) collective-permute-start(bf16[208,128]{1,0:T(8,128)(2,1)S(1)} %get-tuple-element.19), channel_id=1, source_target_pairs={{0,24},{4,28},{8,16},{12,20},{16,8},{20,12},{24,0},{28,4},{1,25},{... | collective-permute-start | bytes 159752 | tf_op jit(solution)/shard_map/ppermute | solution.py:472
  12.9 6.2 %collective-permute-start.7 = (bf16[144,128]{1,0:T(8,128)(2,1)S(1)}, bf16[144,128]{1,0:T(8,128)(2,1)S(1)}, u32[]{:S(2)}, u32[]{:S(2)}) collective-permute-start(bf16[144,128]{1,0:T(8,128)(2,1)S(1)} %forward.3), channel_id=1, source_target_pairs={{0,4},{4,0},{8,12},{12,8},{16,20},{20,16},{24,28},{28,24},{1,5},{5... | collective-permute-start | bytes 110600 | tf_op jit(solution)/shard_map/ppermute | solution.py:491
  14.4 4.6 %collective-permute-start.3 = (bf16[144,128]{1,0:T(8,128)(2,1)S(1)}, bf16[144,128]{1,0:T(8,128)(2,1)S(1)}, u32[]{:S(2)}, u32[]{:S(2)}) collective-permute-start(bf16[144,128]{1,0:T(8,128)(2,1)S(1)} %get-tuple-element.17), channel_id=1, source_target_pairs={{0,8},{4,12},{8,0},{12,4},{16,24},{20,28},{24,16},{28,20},{1,9},{5... | collective-permute-start | bytes 110600 | tf_op jit(solution)/shard_map/ppermute | solution.py:472
  14.6 4.9 %collective-permute-start.6 = (bf16[144,128]{1,0:T(8,128)(2,1)S(1)}, bf16[144,128]{1,0:T(8,128)(2,1)S(1)}, u32[]{:S(2)}, u32[]{:S(2)}) collective-permute-start(bf16[144,128]{1,0:T(8,128)(2,1)S(1)} %get-tuple-element.20), channel_id=1, source_target_pairs={{0,12},{4,8},{8,4},{12,0},{16,28},{20,24},{24,20},{28,16},{1,13},{... | collective-permute-start | bytes 110600 | tf_op jit(solution)/shard_map/ppermute | solution.py:491
  16.4 4.0 %collective-permute-start.8 = (bf16[144,128]{1,0:T(8,128)(2,1)S(1)}, bf16[144,128]{1,0:T(8,128)(2,1)S(1)}, u32[]{:S(2)}, u32[]{:S(2)}) collective-permute-start(bf16[144,128]{1,0:T(8,128)(2,1)S(1)} %forward.4), channel_id=1, source_target_pairs={{0,4},{4,0},{8,12},{12,8},{16,20},{20,16},{24,28},{28,24},{1,5},{5... | collective-permute-start | bytes 110600 | tf_op jit(solution)/shard_map/ppermute | solution.py:491
  17.9 4.0 %collective-permute-start.9 = (bf16[144,128]{1,0:T(8,128)(2,1)S(1)}, bf16[144,128]{1,0:T(8,128)(2,1)S(1)}, u32[]{:S(2)}, u32[]{:S(2)}) collective-permute-start(bf16[144,128]{1,0:T(8,128)(2,1)S(1)} %forward.5), channel_id=1, source_target_pairs={{0,4},{4,0},{8,12},{12,8},{16,20},{20,16},{24,28},{28,24},{1,5},{5... | collective-permute-start | bytes 110600 | tf_op jit(solution)/shard_map/ppermute | solution.py:491
  21.9 1.5 %collective-permute-start.10 = (bf16[8,80,128]{2,1,0:T(8,128)(2,1)S(1)}, bf16[8,80,128]{2,1,0:T(8,128)(2,1)S(1)}, u32[]{:S(2)}, u32[]{:S(2)}) collective-permute-start(bf16[8,80,128]{2,1,0:T(8,128)(2,1)S(1)} %collect.1.refs_8_), channel_id=1, source_target_pairs={{0,1},{1,0},{2,3},{3,2},{4,5},{5,4},{6,7},{7,6},{8,9},{9,8},{10,11... | collective-permute-start | bytes 491528 | tf_op jit(solution)/shard_map/ppermute | solution.py:501
where the time goes:
time: 27.4 us; the launch traced here: 27.2 us
  starting transfers between devices  13.3 us (49%)
  waiting for transfers between devices  6.67 us (24%)
  Pallas kernels  6.59 us (24%)
  between operations  0.68 us (2%)
    ppermute x4, starting transfers between devices, local(): lax.ppermute(forward, 'tm', [(t, t ^ by) for t in range(steps)])  5.91 us
    ppermute x3, starting transfers between devices, local(): lax.ppermute(outgoing[k], 'tm', [(t, t ^ 2 * k) for t in range(steps)])  4.18 us
    pallas_call x1, Pallas kernels, local(): pl.pallas_call(functools.partial(correlate_kernel, seg_count, src_count,...  3.87 us
    ppermute x3, starting transfers between devices, local(): lax.ppermute(picked, 'chan', [(c, c ^ k) for c in range(chan_count)])  3.12 us
    ppermute x3, waiting for transfers between devices, local(): lax.ppermute(picked, 'chan', [(c, c ^ k) for c in range(chan_count)])  3.11 us
    ppermute x4, waiting for transfers between devices, local(): lax.ppermute(forward, 'tm', [(t, t ^ by) for t in range(steps)])  2.82 us
    pallas_call x1, Pallas kernels, local(): pl.pallas_call(functools.partial(filter_kernel, blocks), out_shape=[pltpu...  2.36 us
    ppermute x1, waiting for transfers between devices, local(): lax.ppermute(given, 'chan', [(c, c ^ 1) for c in range(chan_count)])  0.73 us
  transfers between devices with their start and end apart: 11, of which 6 were waited for; matrix products, arithmetic and copies ran while one was open for 0% of the time, Pallas kernels for 0%

commit v1 on v0

--- a/solution.py
+++ b/solution.py
@@ -100,6 +100,12 @@
     ch = rows // steps
     span = raw_len // blocks
     wide = span + LANES
+    small = [
+        pltpu.make_async_copy(taps_hbm, taps_ref, sems.at[blocks]),
+        pltpu.make_async_copy(src_hbm, src_ref, sems.at[blocks + 1]),
+    ]
+    for copy in small:
+        copy.start()
     copies = []
     for b in range(blocks):
         if b == 0:
@@ -116,13 +122,8 @@
             )
         copy.start()
         copies.append(copy)
-    small = [
-        pltpu.make_async_copy(taps_hbm, taps_ref, sems.at[blocks]),
-        pltpu.make_async_copy(src_hbm, src_ref, sems.at[blocks + 1]),
-    ]
     tables = pltpu.make_async_copy(tab_hbm, tab_ref, sems.at[blocks + 2])
-    for copy in [*small, tables]:
-        copy.start()
+    tables.start()
     ext[:rows, :LANES] = jnp.zeros((rows, LANES), ext.dtype)
     weight[...] = jnp.zeros_like(weight)
     for copy in small:
@@ -499,8 +500,8 @@
         name="collect",
     )(*arrived, *passed)
     swapped = lax.ppermute(given, "chan", [(c, c ^ 1) for c in range(chan_count)])
-    block = math.gcd(src_count, 16)
-    count = math.gcd(src_count // block, 2)
+    block = math.gcd(src_count, 8)
+    count = math.gcd(src_count // block, 4)
     state = seg_count * total_rows * SEG * 4
     return pl.pallas_call(
         functools.partial(

time: 27.4 us -> 27.3 us (level)
  no operation moved by 1% of the time
where the time goes in v1:
time: 27.3 us; the launch traced here: 27.1 us
  starting transfers between devices  13.3 us (49%)
  waiting for transfers between devices  6.67 us (24%)
  Pallas kernels  6.48 us (24%)
  between operations  0.68 us (2%)
    ppermute x4, starting transfers between devices, local(): lax.ppermute(forward, 'tm', [(t, t ^ by) for t in range(steps)])  5.91 us
    ppermute x3, starting transfers between devices, local(): lax.ppermute(outgoing[k], 'tm', [(t, t ^ 2 * k) for t in range(steps)])  4.18 us
    pallas_call x1, Pallas kernels, local(): pl.pallas_call(functools.partial(correlate_kernel, seg_count, src_count,...  3.76 us
    ppermute x3, starting transfers between devices, local(): lax.ppermute(picked, 'chan', [(c, c ^ k) for c in range(chan_count)])  3.12 us
    ppermute x3, waiting for transfers between devices, local(): lax.ppermute(picked, 'chan', [(c, c ^ k) for c in range(chan_count)])  3.11 us
    ppermute x4, waiting for transfers between devices, local(): lax.ppermute(forward, 'tm', [(t, t ^ by) for t in range(steps)])  2.82 us
    pallas_call x1, Pallas kernels, local(): pl.pallas_call(functools.partial(filter_kernel, blocks), out_shape=[pltpu...  2.35 us
    ppermute x1, waiting for transfers between devices, local(): lax.ppermute(given, 'chan', [(c, c ^ 1) for c in range(chan_count)])  0.73 us
  transfers between devices with their start and end apart: 11, of which 6 were waited for; matrix products, arithmetic and copies ran while one was open for 0% of the time, Pallas kernels for 0%

profile of v1, /device:TPU:0, one launch (start us, length us, event | category | flops | bytes accessed | tf_op | source)
XLA Modules:
  0.0 27.1 jit_solution(10234654960438380515)
XLA Ops:
  0.0 2.3 %fir.1 = (bf16[8,80,128]{2,1,0:T(8,128)(2,1)S(1)}, bf16[16,640]{1,0:T(8,128)(2,1)S(1)}, bf16[512,2816]{1,0:T(8,128)(2,1)S(1)}) custom-call(s32[1,32]{1,0:T(1,128)} %bitcast.2, f32[1,128]{1,0:T(1,128)} %bitcast.3, bf16[128,5120]{1,0:T(8,128)(2,1)} %raw_ref.1, bf16[512,2816]{1,0:T(8,128)(2,1)} %constant.2.clone.tab_hbm), custom_call_target="tpu_custom_call" | custom-call | tf_op jit(solution)/shard_map/fir/pallas_call | solution.py:437
  2.4 2.4 %collective-permute-start.2 = (bf16[16,640]{1,0:T(8,128)(2,1)S(1)}, bf16[16,640]{1,0:T(8,128)(2,1)S(1)}, u32[]{:S(2)}, u32[]{:S(2)}) collective-permute-start(bf16[16,640]{1,0:T(8,128)(2,1)S(1)} %get-tuple-element.14.refs_0_), channel_id=1, source_target_pairs={{0,3},{1,2},{2,1},{3,0},{4,7},{5,6},{6,5},{7,4},{8,11},{9,10},{10,... | collective-permute-start | bytes 61448 | tf_op jit(solution)/shard_map/ppermute | solution.py:457
  4.8 0.6 %collective-permute-start.1 = (bf16[16,640]{1,0:T(8,128)(2,1)S(1)}, bf16[16,640]{1,0:T(8,128)(2,1)S(1)}, u32[]{:S(2)}, u32[]{:S(2)}) collective-permute-start(bf16[16,640]{1,0:T(8,128)(2,1)S(1)} %get-tuple-element.14.refs_0_), channel_id=1, source_target_pairs={{0,2},{1,3},{2,0},{3,1},{4,6},{5,7},{6,4},{7,5},{8,10},{9,11},{10,... | collective-permute-start | bytes 61448 | tf_op jit(solution)/shard_map/ppermute | solution.py:457
  5.4 0.0 collective-permute-start
  5.5 0.8 %collective-permute-done.2.refs_3_ = bf16[16,640]{1,0:T(8,128)(2,1)S(1)} collective-permute-done((bf16[16,640]{1,0:T(8,128)(2,1)S(1)}, bf16[16,640]{1,0:T(8,128)(2,1)S(1)}, u32[]{:S(2)}, u32[]{:S(2)}) %collective-permute-start.2) | collective-permute-done | bytes 20512 | tf_op jit(solution)/shard_map/ppermute | solution.py:457
  6.3 2.3 %collective-permute-done.1.refs_2_ = bf16[16,640]{1,0:T(8,128)(2,1)S(1)} collective-permute-done((bf16[16,640]{1,0:T(8,128)(2,1)S(1)}, bf16[16,640]{1,0:T(8,128)(2,1)S(1)}, u32[]{:S(2)}, u32[]{:S(2)}) %collective-permute-start.1) | collective-permute-done | bytes 20512 | tf_op jit(solution)/shard_map/ppermute | solution.py:457
  8.6 0.0 collective-permute-done.refs_1_
  8.6 0.3 %arrange.1 = (bf16[208,128]{1,0:T(8,128)(2,1)S(1)}, bf16[144,128]{1,0:T(8,128)(2,1)S(1)}, bf16[208,128]{1,0:T(8,128)(2,1)S(1)}, bf16[208,128]{1,0:T(8,128)(2,1)S(1)}, bf16[144,128]{1,0:T(8,128)(2,1)S(1)}) custom-call(bf16[16,640]{1,0:T(8,128)(2,1)S(1)} %get-tuple-element.14.refs_0_, bf16[16,640]{1,0:T(8,128)(2,1)S(1)} %collective-permute-done.refs_1_, ...), custom_call_target="tpu_custom_call" | custom-call | tf_op jit(solution)/shard_map/arrange/pallas_call | solution.py:461
  8.9 2.6 %collective-permute-start.4 = (bf16[208,128]{1,0:T(8,128)(2,1)S(1)}, bf16[208,128]{1,0:T(8,128)(2,1)S(1)}, u32[]{:S(2)}, u32[]{:S(2)}) collective-permute-start(bf16[208,128]{1,0:T(8,128)(2,1)S(1)} %get-tuple-element.18), channel_id=1, source_target_pairs={{0,16},{4,20},{8,24},{12,28},{16,0},{20,4},{24,8},{28,12},{1,17},{... | collective-permute-start | bytes 159752 | tf_op jit(solution)/shard_map/ppermute | solution.py:473
  11.5 1.3 %collective-permute-start.5 = (bf16[208,128]{1,0:T(8,128)(2,1)S(1)}, bf16[208,128]{1,0:T(8,128)(2,1)S(1)}, u32[]{:S(2)}, u32[]{:S(2)}) collective-permute-start(bf16[208,128]{1,0:T(8,128)(2,1)S(1)} %get-tuple-element.19), channel_id=1, source_target_pairs={{0,24},{4,28},{8,16},{12,20},{16,8},{20,12},{24,0},{28,4},{1,25},{... | collective-permute-start | bytes 159752 | tf_op jit(solution)/shard_map/ppermute | solution.py:473
  12.9 1.5 %collective-permute-start.7 = (bf16[144,128]{1,0:T(8,128)(2,1)S(1)}, bf16[144,128]{1,0:T(8,128)(2,1)S(1)}, u32[]{:S(2)}, u32[]{:S(2)}) collective-permute-start(bf16[144,128]{1,0:T(8,128)(2,1)S(1)} %forward.3), channel_id=1, source_target_pairs={{0,4},{4,0},{8,12},{12,8},{16,20},{20,16},{24,28},{28,24},{1,5},{5... | collective-permute-start | bytes 110600 | tf_op jit(solution)/shard_map/ppermute | solution.py:492
  14.4 0.2 collective-permute-start.3
  14.6 1.7 %collective-permute-start.6 = (bf16[144,128]{1,0:T(8,128)(2,1)S(1)}, bf16[144,128]{1,0:T(8,128)(2,1)S(1)}, u32[]{:S(2)}, u32[]{:S(2)}) collective-permute-start(bf16[144,128]{1,0:T(8,128)(2,1)S(1)} %get-tuple-element.20), channel_id=1, source_target_pairs={{0,12},{4,8},{8,4},{12,0},{16,28},{20,24},{24,20},{28,16},{1,13},{... | collective-permute-start | bytes 110600 | tf_op jit(solution)/shard_map/ppermute | solution.py:492
  16.4 0.0 collective-permute-done.4.block_ref.refs_2_
  16.4 1.5 %collective-permute-start.8 = (bf16[144,128]{1,0:T(8,128)(2,1)S(1)}, bf16[144,128]{1,0:T(8,128)(2,1)S(1)}, u32[]{:S(2)}, u32[]{:S(2)}) collective-permute-start(bf16[144,128]{1,0:T(8,128)(2,1)S(1)} %forward.4), channel_id=1, source_target_pairs={{0,4},{4,0},{8,12},{12,8},{16,20},{20,16},{24,28},{28,24},{1,5},{5... | collective-permute-start | bytes 110600 | tf_op jit(solution)/shard_map/ppermute | solution.py:492
  17.9 0.0 collective-permute-done.5.block_ref.refs_3_
  17.9 1.1 %collective-permute-start.9 = (bf16[144,128]{1,0:T(8,128)(2,1)S(1)}, bf16[144,128]{1,0:T(8,128)(2,1)S(1)}, u32[]{:S(2)}, u32[]{:S(2)}) collective-permute-start(bf16[144,128]{1,0:T(8,128)(2,1)S(1)} %forward.5), channel_id=1, source_target_pairs={{0,4},{4,0},{8,12},{12,8},{16,20},{20,16},{24,28},{28,24},{1,5},{5... | collective-permute-start | bytes 110600 | tf_op jit(solution)/shard_map/ppermute | solution.py:492
  19.0 0.0 collective-permute-done.7.refs_5_
  19.0 0.0 collective-permute-done.3.refs_1_
  19.0 0.4 %collective-permute-done.6.refs_4_ = bf16[144,128]{1,0:T(8,128)(2,1)S(1)} collective-permute-done((bf16[144,128]{1,0:T(8,128)(2,1)S(1)}, bf16[144,128]{1,0:T(8,128)(2,1)S(1)}, u32[]{:S(2)}, u32[]{:S(2)}) %collective-permute-start.6) | collective-permute-done | bytes 36896 | tf_op jit(solution)/shard_map/ppermute | solution.py:492
  19.5 0.8 %collective-permute-done.8.refs_6_ = bf16[144,128]{1,0:T(8,128)(2,1)S(1)} collective-permute-done((bf16[144,128]{1,0:T(8,128)(2,1)S(1)}, bf16[144,128]{1,0:T(8,128)(2,1)S(1)}, u32[]{:S(2)}, u32[]{:S(2)}) %collective-permute-start.8) | collective-permute-done | bytes 36896 | tf_op jit(solution)/shard_map/ppermute | solution.py:492
  20.3 1.5 %collective-permute-done.9.refs_7_ = bf16[144,128]{1,0:T(8,128)(2,1)S(1)} collective-permute-done((bf16[144,128]{1,0:T(8,128)(2,1)S(1)}, bf16[144,128]{1,0:T(8,128)(2,1)S(1)}, u32[]{:S(2)}, u32[]{:S(2)}) %collective-permute-start.9) | collective-permute-done | bytes 36896 | tf_op jit(solution)/shard_map/ppermute | solution.py:492
  21.9 0.1 collective-permute-start.10
  22.6 0.7 %collective-permute-done.10.refs_9_ = bf16[8,80,128]{2,1,0:T(8,128)(2,1)S(1)} collective-permute-done((bf16[8,80,128]{2,1,0:T(8,128)(2,1)S(1)}, bf16[8,80,128]{2,1,0:T(8,128)(2,1)S(1)}, u32[]{:S(2)}, u32[]{:S(2)}) %collective-permute-start.10) | collective-permute-done | bytes 163872 | tf_op jit(solution)/shard_map/ppermute | solution.py:502
  23.3 3.8 %correlate.1 = f32[32,16,384]{2,1,0:T(8,128)} custom-call(s32[1]{0:T(128)S(6)} %copy.6.live_ref, bf16[512,2816]{1,0:T(8,128)(2,1)S(1)} %get-tuple-element.13.tab_ref, bf16[208,128]{1,0:T(8,128)(2,1)S(1)} %get-tuple-element.16.block_ref.refs_0_, bf16[144,128]{1,0:T(8,128)(2,1)S(1)} %collective-permute-done.3.refs_1_, ...), custom_call_target="tpu_custom_call" | custom-call | tf_op jit(solution)/shard_map/correlate/pallas_call | solution.py:506
  (4 shorter events, 0.0 us)
Async XLA Ops:
  2.4 4.0 %collective-permute-start.2 = (bf16[16,640]{1,0:T(8,128)(2,1)S(1)}, bf16[16,640]{1,0:T(8,128)(2,1)S(1)}, u32[]{:S(2)}, u32[]{:S(2)}) collective-permute-start(bf16[16,640]{1,0:T(8,128)(2,1)S(1)} %get-tuple-element.14.refs_0_), channel_id=1, source_target_pairs={{0,3},{1,2},{2,1},{3,0},{4,7},{5,6},{6,5},{7,4},{8,11},{9,10},{10,... | collective-permute-start | bytes 61448 | tf_op jit(solution)/shard_map/ppermute | solution.py:457
  4.8 3.8 %collective-permute-start.1 = (bf16[16,640]{1,0:T(8,128)(2,1)S(1)}, bf16[16,640]{1,0:T(8,128)(2,1)S(1)}, u32[]{:S(2)}, u32[]{:S(2)}) collective-permute-start(bf16[16,640]{1,0:T(8,128)(2,1)S(1)} %get-tuple-element.14.refs_0_), channel_id=1, source_target_pairs={{0,2},{1,3},{2,0},{3,1},{4,6},{5,7},{6,4},{7,5},{8,10},{9,11},{10,... | collective-permute-start | bytes 61448 | tf_op jit(solution)/shard_map/ppermute | solution.py:457
  5.4 3.1 %collective-permute-start = (bf16[16,640]{1,0:T(8,128)(2,1)S(1)}, bf16[16,640]{1,0:T(8,128)(2,1)S(1)}, u32[]{:S(2)}, u32[]{:S(2)}) collective-permute-start(bf16[16,640]{1,0:T(8,128)(2,1)S(1)} %get-tuple-element.14.refs_0_), channel_id=1, source_target_pairs={{0,1},{1,0},{2,3},{3,2},{4,5},{5,4},{6,7},{7,6},{8,9},{9,8},{10,11... | collective-permute-start | bytes 61448 | tf_op jit(solution)/shard_map/ppermute | solution.py:457
  8.9 7.4 %collective-permute-start.4 = (bf16[208,128]{1,0:T(8,128)(2,1)S(1)}, bf16[208,128]{1,0:T(8,128)(2,1)S(1)}, u32[]{:S(2)}, u32[]{:S(2)}) collective-permute-start(bf16[208,128]{1,0:T(8,128)(2,1)S(1)} %get-tuple-element.18), channel_id=1, source_target_pairs={{0,16},{4,20},{8,24},{12,28},{16,0},{20,4},{24,8},{28,12},{1,17},{... | collective-permute-start | bytes 159752 | tf_op jit(solution)/shard_map/ppermute | solution.py:473
  11.5 6.4 %collective-permute-start.5 = (bf16[208,128]{1,0:T(8,128)(2,1)S(1)}, bf16[208,128]{1,0:T(8,128)(2,1)S(1)}, u32[]{:S(2)}, u32[]{:S(2)}) collective-permute-start(bf16[208,128]{1,0:T(8,128)(2,1)S(1)} %get-tuple-element.19), channel_id=1, source_target_pairs={{0,24},{4,28},{8,16},{12,20},{16,8},{20,12},{24,0},{28,4},{1,25},{... | collective-permute-start | bytes 159752 | tf_op jit(solution)/shard_map/ppermute | solution.py:473
  12.9 6.2 %collective-permute-start.7 = (bf16[144,128]{1,0:T(8,128)(2,1)S(1)}, bf16[144,128]{1,0:T(8,128)(2,1)S(1)}, u32[]{:S(2)}, u32[]{:S(2)}) collective-permute-start(bf16[144,128]{1,0:T(8,128)(2,1)S(1)} %forward.3), channel_id=1, source_target_pairs={{0,4},{4,0},{8,12},{12,8},{16,20},{20,16},{24,28},{28,24},{1,5},{5... | collective-permute-start | bytes 110600 | tf_op jit(solution)/shard_map/ppermute | solution.py:492
  14.4 4.6 %collective-permute-start.3 = (bf16[144,128]{1,0:T(8,128)(2,1)S(1)}, bf16[144,128]{1,0:T(8,128)(2,1)S(1)}, u32[]{:S(2)}, u32[]{:S(2)}) collective-permute-start(bf16[144,128]{1,0:T(8,128)(2,1)S(1)} %get-tuple-element.17), channel_id=1, source_target_pairs={{0,8},{4,12},{8,0},{12,4},{16,24},{20,28},{24,16},{28,20},{1,9},{5... | collective-permute-start | bytes 110600 | tf_op jit(solution)/shard_map/ppermute | solution.py:473
  14.6 4.9 %collective-permute-start.6 = (bf16[144,128]{1,0:T(8,128)(2,1)S(1)}, bf16[144,128]{1,0:T(8,128)(2,1)S(1)}, u32[]{:S(2)}, u32[]{:S(2)}) collective-permute-start(bf16[144,128]{1,0:T(8,128)(2,1)S(1)} %get-tuple-element.20), channel_id=1, source_target_pairs={{0,12},{4,8},{8,4},{12,0},{16,28},{20,24},{24,20},{28,16},{1,13},{... | collective-permute-start | bytes 110600 | tf_op jit(solution)/shard_map/ppermute | solution.py:492
  16.4 4.0 %collective-permute-start.8 = (bf16[144,128]{1,0:T(8,128)(2,1)S(1)}, bf16[144,128]{1,0:T(8,128)(2,1)S(1)}, u32[]{:S(2)}, u32[]{:S(2)}) collective-permute-start(bf16[144,128]{1,0:T(8,128)(2,1)S(1)} %forward.4), channel_id=1, source_target_pairs={{0,4},{4,0},{8,12},{12,8},{16,20},{20,16},{24,28},{28,24},{1,5},{5... | collective-permute-start | bytes 110600 | tf_op jit(solution)/shard_map/ppermute | solution.py:492
  17.9 4.0 %collective-permute-start.9 = (bf16[144,128]{1,0:T(8,128)(2,1)S(1)}, bf16[144,128]{1,0:T(8,128)(2,1)S(1)}, u32[]{:S(2)}, u32[]{:S(2)}) collective-permute-start(bf16[144,128]{1,0:T(8,128)(2,1)S(1)} %forward.5), channel_id=1, source_target_pairs={{0,4},{4,0},{8,12},{12,8},{16,20},{20,16},{24,28},{28,24},{1,5},{5... | collective-permute-start | bytes 110600 | tf_op jit(solution)/shard_map/ppermute | solution.py:492
  21.9 1.5 %collective-permute-start.10 = (bf16[8,80,128]{2,1,0:T(8,128)(2,1)S(1)}, bf16[8,80,128]{2,1,0:T(8,128)(2,1)S(1)}, u32[]{:S(2)}, u32[]{:S(2)}) collective-permute-start(bf16[8,80,128]{2,1,0:T(8,128)(2,1)S(1)} %collect.1.refs_8_), channel_id=1, source_target_pairs={{0,1},{1,0},{2,3},{3,2},{4,5},{5,4},{6,7},{7,6},{8,9},{9,8},{10,11... | collective-permute-start | bytes 491528 | tf_op jit(solution)/shard_map/ppermute | solution.py:502
